TPU v7x, 512 devices: a whole 4x8x8 slice. The times are simulated.
512 devices in a mesh: members: 8 (over y), bands: 64 (over z, x, core).
Axes of the slice: x: 4, y: 8, z: 8, core: 2. Of those that a mesh axis runs over, the one named last changes fastest.
Arguments:
- ensemble: float32 [128, 1024, 128], P('members', 'bands'), may hold values from -6 to 6
- neighbours: int32 [1024, 4], P('bands'), may hold values from 0 to 1023, as said below
- regime: int32 [1024], P('bands'), may hold values from 0 to 3
- norm_gain: float32 [128], replicated, may hold values from 0.25 to 1.75
- up_weight: bfloat16 [4, 128, 512], replicated, may hold values from -0.5 to 0.5
- down_weight: bfloat16 [4, 512, 128], replicated, may hold values from -0.25 to 0.25
- vertical_modes: float32 [4, 128], replicated, may hold values from -3 to 3
- obs_col: int32 [16384], P('bands'), may hold values from 0 to 1023, as said below
- obs_lev: int32 [16384], P('bands'), may hold values from 0 to 127
- obs_val: float32 [16384], P('bands'), may hold values from -9 to 9
- obs_err: float32 [16384], P('bands'), may hold values from 0.3 to 1
Outputs:
- analysis: float32 [128, 1024, 128], P('members', 'bands')
Inputs may be any that keep to these rules, and one draw needn't show every extreme that they name: `neighbours`: every neighbour of column c lies within 8 columns of c. `obs_col`: the observations at positions b * 256 to (b + 1) * 256 - 1 lie in columns b * 16 to (b + 1) * 16 - 1.
All inputs are finite; a program needn't handle non-finite values.
Results may differ from a plain program's by a relative error of at most 0.0034.
Values sent between devices are 32-bit elements; how exact they have to be, the bound alone decides.
No kernel may reach another device: no remote copies, remote signals or barrier semaphores. Data moves between devices by JAX's collectives and lax.ppermute only.
A program may use at most 64 MiB of HBM per device.

v0:
```python
import math
import jax
import jax.numpy as jnp
from jax import lax
from jax.sharding import PartitionSpec as P

E = 4
L = 4
NB = 4
HALO = 8
NS_ITERS = 4
highest = lax.Precision.HIGHEST


def extended(block, sides, width):
    for axis, dim in sides:
        count = lax.axis_size(axis)
        forward = [(i, i + 1) for i in range(count - 1)]
        backward = [(target, source) for source, target in forward]
        low = lax.ppermute(
            lax.slice_in_dim(block, block.shape[dim] - width, None, axis=dim), axis, forward
        )
        high = lax.ppermute(lax.slice_in_dim(block, 0, width, axis=dim), axis, backward)
        block = jnp.concatenate([low, block, high], axis=dim)
    return block


def analysis_coefficients(gram_matrix, cross_terms, drive_terms):
    order_k = gram_matrix.shape[0]
    identity = jnp.eye(order_k, dtype=jnp.float32)
    system = identity + gram_matrix
    norm_scale = jnp.sqrt(jnp.sum(system * system))
    iterate = system / norm_scale
    inverse = identity
    for sweep_index in range(NS_ITERS):
        if sweep_index == 0:
            product = iterate
        else:
            product = jnp.dot(inverse, iterate, precision=highest)
        factor = 1.5 * identity - 0.5 * product
        if sweep_index + 1 < NS_ITERS:
            iterate = jnp.dot(iterate, factor, precision=highest)
        if sweep_index == 0:
            inverse = factor
        else:
            inverse = jnp.dot(factor, inverse, precision=highest)
    root_factor = inverse / jnp.sqrt(norm_scale)
    weights_matrix = jnp.dot(root_factor, root_factor, precision=highest)
    mean_weights = jnp.dot(weights_matrix, drive_terms, precision=highest)
    return mean_weights[:, None] - 0.5 * jnp.dot(weights_matrix, cross_terms, precision=highest)


def per_device(
    ensemble,
    neighbours,
    regime,
    norm_gain,
    up_weight,
    down_weight,
    vertical_modes,
    obs_col,
    obs_lev,
    obs_val,
    obs_err,
):
    member_deviation, column_deviation, level_count = ensemble.shape
    band_index = lax.axis_index("bands")
    group_index = lax.axis_index("members")
    widened = extended(ensemble, (("bands", 1),), HALO)
    local_nb = neighbours - band_index * column_deviation + HALO
    summed_nb = jnp.zeros_like(ensemble)
    for which in range(NB):
        summed_nb = summed_nb + widened[:, local_nb[:, which], :]
    filtered_profile = ensemble + 0.5 * (0.25 * summed_nb - ensemble)
    flat = filtered_profile.reshape(member_deviation * column_deviation, level_count)
    inv_rms = lax.rsqrt(jnp.mean(flat * flat, axis=1, keepdims=True) + 1e-05)
    normed = (flat * inv_rms * norm_gain).astype(jnp.bfloat16)
    hidden = jax.nn.silu(
        jnp.einsum("rl,elf->erf", normed, up_weight, preferred_element_type=jnp.float32)
    ).astype(jnp.bfloat16)
    expert_out = jnp.einsum("erf,efl->erl", hidden, down_weight, preferred_element_type=jnp.float32)
    selected = regime[None, :] == jnp.arange(E, dtype=jnp.int32)[:, None]
    selected = jnp.tile(selected, (1, member_deviation))
    time_derivative = jnp.sum(jnp.where(selected[:, :, None], expert_out, 0.0), axis=0)
    predicted_vector = filtered_profile + time_derivative.reshape(
        member_deviation, column_deviation, level_count
    )
    vertical_lattice = lax.all_to_all(
        predicted_vector, "members", split_axis=1, concat_axis=0, tiled=True
    )
    share_cols = vertical_lattice.shape[1]
    average_sample_vector = jnp.mean(vertical_lattice, axis=0)
    sample_anomaly = vertical_lattice - average_sample_vector
    local_col = obs_col - band_index * column_deviation - group_index * share_cols
    inside = (local_col >= 0) & (local_col < share_cols)
    clipped = jnp.clip(local_col, 0, share_cols - 1)
    sampled = sample_anomaly[:, clipped, obs_lev]
    obs_pert = jnp.where(inside[None, :], sampled / obs_err, 0.0).T
    innovation = jnp.where(
        inside, (obs_val - average_sample_vector[clipped, obs_lev]) / obs_err, 0.0
    )
    members_all = obs_pert.shape[1]
    order_k = L * members_all
    obs_rows = obs_pert.shape[0]
    modulated = (vertical_modes[:, obs_lev].T[:, :, None] * obs_pert[:, None, :]).reshape(
        obs_rows, order_k
    ) / math.sqrt(order_k - 1)
    cross_part = jnp.dot(modulated.T, obs_pert, precision=highest)
    drive_part = jnp.dot(modulated.T, innovation, precision=highest)
    gram_part = jnp.dot(modulated.T, modulated, precision=highest)
    gram_matrix, cross_terms, drive_terms = lax.psum(
        (gram_part, cross_part, drive_part), ("members", "bands")
    )
    coefficients = analysis_coefficients(gram_matrix, cross_terms, drive_terms)
    coeff_modes = coefficients.reshape(L, members_all, members_all)
    update_correction = jnp.zeros_like(vertical_lattice)
    for layer in range(L):
        mixed = jnp.einsum("acv,ab->bcv", sample_anomaly, coeff_modes[layer], precision=highest)
        update_correction = update_correction + vertical_modes[layer][None, None, :] * mixed
    analysed = vertical_lattice + update_correction / math.sqrt(order_k - 1)
    return lax.all_to_all(analysed, "members", split_axis=0, concat_axis=1, tiled=True)


def solution(mesh):
    in_specs = (
        P("members", "bands", None),
        P("bands", None),
        P("bands"),
        P(),
        P(),
        P(),
        P(),
        P("bands"),
        P("bands"),
        P("bands"),
        P("bands"),
    )
    out_specs = P("members", "bands", None)
    return jax.shard_map(
        per_device, mesh=mesh, in_specs=in_specs, out_specs=out_specs, check_vma=False
    )
```

profile of v0, /device:TPU:8, one launch (start us, length us, event | category | flops | bytes accessed | tf_op | source)
XLA Modules:
  0.0 368.7 jit_solution(5785162211855150360)
XLA Ops:
  6.5 0.9 fusion.62
  7.5 1.9 collective-permute-start
  9.4 1.3 collective-permute-start.1
  11.4 0.7 subtract_add_fusion
  12.2 0.8 copy.73
  13.0 0.9 constant_dynamic-update-slice_fusion.1
  16.9 1.0 fusion.6
  17.9 0.7 copy_add_fusion
  18.6 8.6 %all-to-all-start = ((f32[16,16,128]{2,0,1:T(8,128)}), f32[16,16,128]{2,0,1:T(8,128)S(1)}, u32[]{:S(2)}, u32[]{:S(2)}) async-start(f32[16,16,128]{2,0,1:T(8,128)} %copy_add_fusion), calls=%async_computation | async-start | bytes 262144 | tf_op jit(solution)/shard_map/all_to_all | solution.py:88
  27.3 0.7 gather_fusion.4
  28.0 8.0 %all-to-all-done = f32[16,16,128]{2,0,1:T(8,128)S(1)} async-done(((f32[16,16,128]{2,0,1:T(8,128)}), f32[16,16,128]{2,0,1:T(8,128)S(1)}, u32[]{:S(2)}, u32[]{:S(2)}) %all-to-all-start) | async-done | bytes 131104 | tf_op jit(solution)/shard_map/all_to_all | solution.py:88
  36.1 2.4 gather_fusion.6
  38.6 1.9 gather_fusion.5
  41.1 1.7 fusion.17
  42.8 2.1 fusion.19
  45.9 104.2 %psum.22 = f32[512]{0:T(512)S(1)} all-reduce(f32[512]{0:T(512)S(1)} %bitcast.136), channel_id=1, replica_groups=mesh['members'=8,'bands'=64] {'members','bands'}, use_global_device_ids=true, to_apply=%region_5.6 | all-reduce | flops 512 | bytes 4096 | tf_op jit(solution)/shard_map/psum | solution.py:111
  150.2 169.8 %all-reduce.3.cloned.1.call-done = (f32[512,512]{1,0:T(8,128)}, f32[512,128]{1,0:T(8,128)}) async-done(((f32[512,512]{1,0:T(8,128)}, f32[512,128]{1,0:T(8,128)}), (f32[512,512]{1,0:T(8,128)}, f32[512,128]{1,0:T(8,128)})) %all-reduce.3.cloned.1.call-update) | async-done | bytes 1310736 | tf_op jit(solution)/shard_map/psum | solution.py:111
  320.0 2.2 multiply_reduce_fusion
  322.9 2.0 fusion.14
  324.9 2.0 select_subtract_fusion.2
  326.9 2.0 fusion.13
  328.9 1.8 fusion.63
  330.8 1.9 select_subtract_fusion.1
  332.6 1.8 fusion.64
  334.5 2.1 fusion.65
  336.6 1.8 select_subtract_fusion
  338.4 1.8 convolution_divide_fusion
  340.3 1.8 fusion.66
  342.1 1.0 fusion.67
  343.1 1.0 fusion.7
  345.5 15.6 %all_to_all.36 = f32[128,2,128]{2,1,0:T(2,128)S(1)} all-to-all(f32[128,2,128]{2,1,0:T(2,128)S(1)} %copy.79), channel_id=1, replica_groups=mesh['members'=8,'bands'=64] {'members'}, dimensions={0} | all-to-all | bytes 262144 | tf_op jit(solution)/shard_map/all_to_all | solution.py:121
  361.2 0.7 copy.80
  (64 shorter events, 6.7 us)
Async XLA Ops:
  6.5 10.3 %copy-start = (bf16[4,512,128]{2,1,0:T(8,128)(2,1)S(1)}, bf16[4,512,128]{2,1,0:T(8,128)(2,1)}, u32[]{:S(2)}) copy-start(bf16[4,512,128]{2,1,0:T(8,128)(2,1)} %param.16) | copy-start | bytes 1572868
  7.5 8.8 %copy-start.1 = (f32[16,16,128]{2,1,0:T(8,128)S(1)}, f32[16,16,128]{2,1,0:T(8,128)}, u32[]{:S(2)}) copy-start(f32[16,16,128]{2,1,0:T(8,128)} %param.11) | copy-start | bytes 393220
  7.5 5.5 %collective-permute-start = (f32[16,8,128]{2,0,1:T(8,128)S(1)}, f32[16,8,128]{2,0,1:T(8,128)S(1)}, u32[]{:S(2)}, u32[]{:S(2)}) collective-permute-start(f32[16,8,128]{2,0,1:T(8,128)S(1)} %copy.107), channel_id=1, source_target_pairs={{0,1},{1,2},{2,3},{3,4},{4,5},{5,6},{6,7},{7,8},{8,9},{9,10},{10,1... | collective-permute-start | bytes 196616 | tf_op jit(solution)/shard_map/ppermute | solution.py:20
  9.4 4.6 %collective-permute-start.1 = (f32[16,8,128]{2,0,1:T(8,128)S(1)}, f32[16,8,128]{2,0,1:T(8,128)S(1)}, u32[]{:S(2)}, u32[]{:S(2)}) collective-permute-start(f32[16,8,128]{2,0,1:T(8,128)S(1)} %copy.108), channel_id=1, source_target_pairs={{1,0},{2,1},{3,2},{4,3},{5,4},{6,5},{7,6},{8,7},{9,8},{10,9},{11,1... | collective-permute-start | bytes 196616 | tf_op jit(solution)/shard_map/ppermute | solution.py:23
  14.0 2.7 copy-start.9
  14.6 2.2 copy-start.10
  16.8 10.4 %copy-start.6 = (s32[256]{0:T(256)S(1)}, s32[256]{0:T(256)}, u32[]{:S(2)}) copy-start(s32[256]{0:T(256)} %param.18) | copy-start | bytes 3076
  16.8 10.4 %copy-start.7 = (s32[256]{0:T(256)S(1)}, s32[256]{0:T(256)}, u32[]{:S(2)}) copy-start(s32[256]{0:T(256)} %param.19) | copy-start | bytes 3076
  18.6 17.4 %all-to-all-start = ((f32[16,16,128]{2,0,1:T(8,128)}), f32[16,16,128]{2,0,1:T(8,128)S(1)}, u32[]{:S(2)}, u32[]{:S(2)}) async-start(f32[16,16,128]{2,0,1:T(8,128)} %copy_add_fusion), calls=%async_computation | async-start | bytes 262144 | tf_op jit(solution)/shard_map/all_to_all | solution.py:88
  27.2 292.8 %all-reduce.3.cloned.1.call-start = ((), (), s32[]{:S(2)}) async-start(), calls=%async_computation.2 | async-start | bytes 2621440 | tf_op jit(solution)/shard_map/psum | solution.py:111
  38.5 2.1 copy-start.5
  38.5 2.1 copy-start.8
  44.8 0.7 copy-start.4
  320.0 2.9 copy-start.2
  342.1 1.0 copy-start.3
Sparse Core Ops, SparseCore 0:
  45.0 274.9 all-reduce.2
where the time goes:
time: 369 us
  waiting for transfers between devices  178 us (48%)
  blocking collectives  120 us (33%)
  matrix products  27.5 us (7%)
  between operations  14.6 us (4%)
  local copies, waits for them, and re-layouts  11.9 us (3%)
  starting transfers between devices  11.8 us (3%)
  other arithmetic  5.08 us (1%)
    psum x1, waiting for transfers between devices, per_device(): lax.psum((gram_part, cross_part, drive_part), ('members', 'bands'))  170 us
    psum x1, blocking collectives, per_device(): lax.psum((gram_part, cross_part, drive_part), ('members', 'bands'))  104 us
    all_to_all x1, blocking collectives, per_device(): lax.all_to_all(analysed, 'members', split_axis=0, concat_axis=1, tiled=True)  15.6 us
    all_to_all x1, starting transfers between devices, per_device(): lax.all_to_all(predicted_vector, 'members', split_axis=1, concat_axis=0,...  8.65 us
    all_to_all x1, waiting for transfers between devices, per_device(): lax.all_to_all(predicted_vector, 'members', split_axis=1, concat_axis=0,...  7.98 us
  transfers between devices with their start and end apart: 4, of which 2 were waited for; matrix products, arithmetic and copies ran while one was open for 1% of the time, Pallas kernels for 0%

commit v1 on v0

--- a/solution.py
+++ b/solution.py
@@ -109,7 +109,7 @@
     drive_part = jnp.dot(modulated.T, innovation, precision=highest)
     gram_part = jnp.dot(modulated.T, modulated, precision=highest)
     gram_matrix, cross_terms, drive_terms = lax.psum(
-        (gram_part, cross_part, drive_part), ("members", "bands")
+        lax.psum((gram_part, cross_part, drive_part), "bands"), "members"
     )
     coefficients = analysis_coefficients(gram_matrix, cross_terms, drive_terms)
     coeff_modes = coefficients.reshape(L, members_all, members_all)

time: 369 us -> 436 us (1.18)
  blocking collectives: 120 us -> 156 us
  waiting for transfers between devices: 178 us -> 209 us
    psum x1 -> x2, blocking collectives: 104 us -> 142 us  [the longest x1 126 us: per_device(): lax.psum((gram_part, cross_part, drive_part), 'bands')]
    psum x1 -> x2, waiting for transfers between devices: 170 us -> 201 us  [the longest x1 201 us: per_device(): lax.psum((gram_part, cross_part, drive_part), 'bands')]
  transfers between devices with their start and end apart: 4 -> 5, of which waited for: 2 -> 2; matrix products, arithmetic and copies ran while one was open for 1% -> 1% of each run, Pallas kernels for 0% -> 0%
where the time goes in v1:
time: 436 us; the launch traced here: 435 us
  waiting for transfers between devices  209 us (48%)
  blocking collectives  156 us (36%)
  matrix products  27.5 us (6%)
  between operations  14.7 us (3%)
  starting transfers between devices  11.9 us (3%)
  local copies, waits for them, and re-layouts  11.3 us (3%)
  other arithmetic  5.08 us (1%)
    psum x1, waiting for transfers between devices, per_device(): lax.psum((gram_part, cross_part, drive_part), 'bands')  201 us
    psum x1, blocking collectives, per_device(): lax.psum((gram_part, cross_part, drive_part), 'bands')  126 us
    psum x1, blocking collectives, per_device(): lax.psum(lax.psum((gram_part, cross_part, drive_part), 'bands'), 'members')  15.9 us
    all_to_all x1, blocking collectives, per_device(): lax.all_to_all(analysed, 'members', split_axis=0, concat_axis=1, tiled=True)  13.7 us
  transfers between devices with their start and end apart: 5, of which 2 were waited for; matrix products, arithmetic and copies ran while one was open for 1% of the time, Pallas kernels for 0%

profile of v1, /device:TPU:8, one launch (start us, length us, event | category | flops | bytes accessed | tf_op | source)
XLA Modules:
  0.0 435.4 jit_solution(16870338438022388290)
XLA Ops:
  6.5 0.9 fusion.62
  7.5 1.9 collective-permute-start
  9.4 1.3 collective-permute-start.1
  12.2 0.8 copy.73
  13.0 0.9 constant_dynamic-update-slice_fusion.1
  16.9 1.0 fusion.6
  17.9 0.7 copy_add_fusion
  18.6 8.6 %all-to-all-start = ((f32[16,16,128]{2,0,1:T(8,128)}), f32[16,16,128]{2,0,1:T(8,128)S(1)}, u32[]{:S(2)}, u32[]{:S(2)}) async-start(f32[16,16,128]{2,0,1:T(8,128)} %copy_add_fusion), calls=%async_computation | async-start | bytes 262144 | tf_op jit(solution)/shard_map/all_to_all | solution.py:88
  27.3 0.7 gather_fusion.4
  28.0 8.0 %all-to-all-done = f32[16,16,128]{2,0,1:T(8,128)S(1)} async-done(((f32[16,16,128]{2,0,1:T(8,128)}), f32[16,16,128]{2,0,1:T(8,128)S(1)}, u32[]{:S(2)}, u32[]{:S(2)}) %all-to-all-start) | async-done | bytes 131104 | tf_op jit(solution)/shard_map/all_to_all | solution.py:88
  36.1 2.4 gather_fusion.6
  38.6 1.9 gather_fusion.5
  41.1 1.7 fusion.17
  42.7 2.1 fusion.19
  44.9 200.9 %all-reduce.5.cloned.1.call-done = (f32[512,512]{1,0:T(8,128)}, f32[512,128]{1,0:T(8,128)}) async-done(((f32[512,512]{1,0:T(8,128)}, f32[512,128]{1,0:T(8,128)}), (f32[512,512]{1,0:T(8,128)}, f32[512,128]{1,0:T(8,128)})) %all-reduce.5.cloned.1.call-update) | async-done | bytes 1310736 | tf_op jit(solution)/shard_map/psum | solution.py:112
  246.3 126.5 %psum.44 = f32[512]{0:T(512)S(1)} all-reduce(f32[512]{0:T(512)S(1)} %bitcast.136), channel_id=1, replica_groups=mesh['members'=8,'bands'=64] {'bands'}, use_global_device_ids=true, to_apply=%region_6.7 | all-reduce | flops 512 | bytes 4096 | tf_op jit(solution)/shard_map/psum | solution.py:112
  372.8 15.9 %psum.45 = f32[512]{0:T(512)S(1)} all-reduce(f32[512]{0:T(512)S(1)} %psum.44), channel_id=1, replica_groups=mesh['members'=8,'bands'=64] {'members'}, use_global_device_ids=true, to_apply=%region_7.8 | all-reduce | flops 512 | bytes 4096 | tf_op jit(solution)/shard_map/psum | solution.py:111
  388.7 2.2 multiply_reduce_fusion
  391.6 2.0 fusion.14
  393.6 2.0 select_subtract_fusion.2
  395.6 2.0 fusion.13
  397.6 1.8 fusion.63
  399.4 1.9 select_subtract_fusion.1
  401.3 1.8 fusion.64
  403.1 2.1 fusion.65
  405.2 1.8 select_subtract_fusion
  407.1 1.9 convolution_divide_fusion
  409.0 1.8 fusion.66
  410.8 1.0 fusion.67
  411.8 1.0 fusion.7
  414.2 13.7 %all_to_all.36 = f32[128,2,128]{2,1,0:T(2,128)S(1)} all-to-all(f32[128,2,128]{2,1,0:T(2,128)S(1)} %copy.79), channel_id=1, replica_groups=mesh['members'=8,'bands'=64] {'members'}, dimensions={0} | all-to-all | bytes 262144 | tf_op jit(solution)/shard_map/all_to_all | solution.py:121
  427.9 0.7 copy.80
  (68 shorter events, 6.8 us)
Async XLA Ops:
  6.5 10.3 %copy-start = (bf16[4,512,128]{2,1,0:T(8,128)(2,1)S(1)}, bf16[4,512,128]{2,1,0:T(8,128)(2,1)}, u32[]{:S(2)}) copy-start(bf16[4,512,128]{2,1,0:T(8,128)(2,1)} %param.16) | copy-start | bytes 1572868
  7.5 8.8 %copy-start.1 = (f32[16,16,128]{2,1,0:T(8,128)S(1)}, f32[16,16,128]{2,1,0:T(8,128)}, u32[]{:S(2)}) copy-start(f32[16,16,128]{2,1,0:T(8,128)} %param.11) | copy-start | bytes 393220
  7.5 5.5 %collective-permute-start = (f32[16,8,128]{2,0,1:T(8,128)S(1)}, f32[16,8,128]{2,0,1:T(8,128)S(1)}, u32[]{:S(2)}, u32[]{:S(2)}) collective-permute-start(f32[16,8,128]{2,0,1:T(8,128)S(1)} %copy.107), channel_id=1, source_target_pairs={{0,1},{1,2},{2,3},{3,4},{4,5},{5,6},{6,7},{7,8},{8,9},{9,10},{10,1... | collective-permute-start | bytes 196616 | tf_op jit(solution)/shard_map/ppermute | solution.py:20
  9.4 4.6 %collective-permute-start.1 = (f32[16,8,128]{2,0,1:T(8,128)S(1)}, f32[16,8,128]{2,0,1:T(8,128)S(1)}, u32[]{:S(2)}, u32[]{:S(2)}) collective-permute-start(f32[16,8,128]{2,0,1:T(8,128)S(1)} %copy.108), channel_id=1, source_target_pairs={{1,0},{2,1},{3,2},{4,3},{5,4},{6,5},{7,6},{8,7},{9,8},{10,9},{11,1... | collective-permute-start | bytes 196616 | tf_op jit(solution)/shard_map/ppermute | solution.py:23
  14.0 2.7 copy-start.9
  14.6 2.2 copy-start.10
  16.8 10.4 %copy-start.6 = (s32[256]{0:T(256)S(1)}, s32[256]{0:T(256)}, u32[]{:S(2)}) copy-start(s32[256]{0:T(256)} %param.18) | copy-start | bytes 3076
  16.8 10.4 %copy-start.7 = (s32[256]{0:T(256)S(1)}, s32[256]{0:T(256)}, u32[]{:S(2)}) copy-start(s32[256]{0:T(256)} %param.19) | copy-start | bytes 3076
  18.6 17.4 %all-to-all-start = ((f32[16,16,128]{2,0,1:T(8,128)}), f32[16,16,128]{2,0,1:T(8,128)S(1)}, u32[]{:S(2)}, u32[]{:S(2)}) async-start(f32[16,16,128]{2,0,1:T(8,128)} %copy_add_fusion), calls=%async_computation | async-start | bytes 262144 | tf_op jit(solution)/shard_map/all_to_all | solution.py:88
  27.2 218.6 %all-reduce.5.cloned.1.call-start = ((), (), s32[]{:S(2)}) async-start(), calls=%async_computation.2 | async-start | bytes 2621440 | tf_op jit(solution)/shard_map/psum | solution.py:112
  38.5 2.1 copy-start.5
  38.5 2.1 copy-start.8
  44.8 201.0 %copy-start.4 = (f32[4,128]{1,0:T(4,128)S(1)}, f32[4,128]{1,0:T(4,128)}, u32[]{:S(2)}) copy-start(f32[4,128]{1,0:T(4,128)} %param.17) | copy-start | bytes 6148
  44.8 343.8 %all-reduce.7.cloned.1.call-start = ((), (), s32[]{:S(2)}) async-start(), calls=%async_computation.3 | async-start | bytes 2621440 | tf_op jit(solution)/shard_map/psum | solution.py:111
  388.7 2.9 copy-start.2
  410.8 1.0 copy-start.3
Sparse Core Ops, SparseCore 0:
  45.0 200.8 all-reduce.4
  248.4 80.0 all-reduce.6
